TPU v7x, 512 devices: a whole 4x4x16 slice. The times are simulated.
512 devices in a mesh: req: 64 (over x, z), kv: 8 (over y, core).
Axes of the slice: x: 4, y: 4, z: 16, core: 2. Of those that a mesh axis runs over, the one named last changes fastest.
Arguments:
- queries: bfloat16 [1024, 8, 8192], P(('req', 'kv')), may hold values from -6 to 6
- new_keys: bfloat16 [1024, 8, 1024], P(('req', 'kv')), may hold values from -6 to 6
- new_values: bfloat16 [1024, 8, 1024], P(('req', 'kv')), may hold values from -6 to 6
- suffix_keys: bfloat16 [1024, 64, 1024], P('req', None, 'kv'), may hold values from -6 to 6
- suffix_values: bfloat16 [1024, 64, 1024], P('req', None, 'kv'), may hold values from -6 to 6
- suffix_len: int32 [1024], P('req'), may hold values from 1 to 64, 32768 in all
- prompt_keys: bfloat16 [128, 128, 1024], P('req', None, 'kv'), may hold values from -6 to 6
- prompt_values: bfloat16 [128, 128, 1024], P('req', None, 'kv'), may hold values from -6 to 6
- parent: int32 [128], P('req'), may hold values from -1 to 0, as said below
- prompt_owner: int32 [1024], P('req'), may hold values from 0 to 63, as said below
- prompt_node: int32 [1024], P('req'), may hold values from 0 to 1
Outputs:
- attended: bfloat16 [1024, 8, 8192], P(('req', 'kv'))
Inputs may be any that keep to these rules, and one draw needn't show every extreme that they name: `prompt_owner`: among the 16 requests of one device of req, no owner appears more than 2 times; one owner, the same for every device, appears exactly 2 times on each device. Within each device's 2 blocks the parent of block j is -1 or a block j' < j of the same device; block 0 is always a root.
All inputs are finite; a program needn't handle non-finite values. No bound on the sum of `suffix_len` on one device may be relied on, other than what follows from the above.
Results may differ from a plain program's by a relative error of at most 0.0043.
Values may be sent and summed in bfloat16 or wider, within the bound.
A program may use at most 64 MiB of HBM per device.

v0:
```python
import math

import jax
import jax.numpy as jnp
from jax import lax
from jax.sharding import PartitionSpec as P

HD = 128


def ancestry(tree_parent):
    width_nodes = tree_parent.shape[-1]
    node_ids = jnp.arange(width_nodes, dtype=jnp.int32)
    current = jnp.broadcast_to(node_ids, tree_parent.shape)
    ancestors = jnp.zeros(tree_parent.shape + (width_nodes,), jnp.float32)
    for depth_step in range(width_nodes):
        at_node = current[..., None] == node_ids
        ancestors = jnp.maximum(ancestors, at_node.astype(jnp.float32))
        upward = jnp.sum(jnp.where(at_node, tree_parent[..., None, :], 0), axis=-1)
        current = jnp.where(current >= 0, upward, -1)
    return ancestors


def merge_parts(prompt_out, prompt_lse, own_out, own_lse):
    highest = jnp.maximum(prompt_lse, own_lse)
    prompt_weight = jnp.exp(prompt_lse - highest)
    own_weight = jnp.exp(own_lse - highest)
    mixed = prompt_weight[..., None] * prompt_out + own_weight[..., None] * own_out
    return mixed / (prompt_weight + own_weight)[..., None]


def prompt_partial(got_queries, got_nodes, pool_keys, pool_values, ancestors, kv_local):
    lead_src, lead_slot, step_count, feature_width = got_queries.shape
    slot_rows = lead_src * lead_slot
    block_total = ancestors.shape[0]
    scaling = 1.0 / math.sqrt(HD)
    queries_split = got_queries.reshape(slot_rows, step_count, kv_local, -1, HD)
    block_keys = pool_keys.reshape(block_total, -1, kv_local, HD)
    block_values = pool_values.reshape(block_total, -1, kv_local, HD)
    chosen = (
        got_nodes.reshape(slot_rows)[:, None] == jnp.arange(block_total, dtype=jnp.int32)[None, :]
    )
    live_blocks = jnp.sum(jnp.where(chosen[:, :, None], ancestors[None], 0.0), axis=1) > 0.5
    usable = live_blocks[:, None, None, :, None]
    outputs = []
    lse_list = []
    for step_index in range(step_count):
        scores = (
            jnp.einsum(
                "cgjd,bwgd->cgjbw",
                queries_split[:, step_index],
                block_keys,
                preferred_element_type=jnp.float32,
            )
            * scaling
        )
        highest = jnp.max(jnp.where(usable, scores, -jnp.inf), axis=(3, 4))
        weights = jnp.where(usable, jnp.exp(scores - highest[..., None, None]), 0.0)
        weight_sum = jnp.sum(weights, axis=(3, 4))
        numerator = jnp.einsum(
            "cgjbw,bwgd->cgjd",
            weights.astype(jnp.bfloat16),
            block_values,
            preferred_element_type=jnp.float32,
        )
        outputs.append(numerator / weight_sum[..., None])
        lse_list.append(highest + jnp.log(weight_sum))
    prompt_out = jnp.stack(outputs, axis=1).reshape(lead_src, lead_slot, step_count, -1, HD)
    prompt_lse = jnp.stack(lse_list, axis=1).reshape(lead_src, lead_slot, step_count, -1)
    return (prompt_out, prompt_lse)


def own_partial(
    head_queries, suffix_keys, suffix_values, fresh_keys, fresh_values, lengths, kv_local
):
    row_count, step_count, feature_width = head_queries.shape
    scaling = 1.0 / math.sqrt(HD)
    queries_split = head_queries.reshape(row_count, step_count, kv_local, -1, HD)
    own_keys = suffix_keys.reshape(row_count, -1, kv_local, HD)
    own_values = suffix_values.reshape(row_count, -1, kv_local, HD)
    new_keys_split = fresh_keys.reshape(row_count, step_count, kv_local, HD)
    new_values_split = fresh_values.reshape(row_count, step_count, kv_local, HD)
    slot_total = own_keys.shape[1]
    suffix_scores = (
        jnp.einsum("rtgjd,rkgd->rtgjk", queries_split, own_keys, preferred_element_type=jnp.float32)
        * scaling
    )
    fresh_scores = (
        jnp.einsum(
            "rtgjd,rkgd->rtgjk", queries_split, new_keys_split, preferred_element_type=jnp.float32
        )
        * scaling
    )
    suffix_ok = (jnp.arange(slot_total, dtype=jnp.int32)[None, :] < lengths[:, None])[
        :, None, None, None, :
    ]
    step_pos = jnp.arange(step_count, dtype=jnp.int32)
    fresh_ok = (step_pos[None, :] <= step_pos[:, None])[None, :, None, None, :]
    own_high = jnp.maximum(
        jnp.max(jnp.where(suffix_ok, suffix_scores, -jnp.inf), axis=-1),
        jnp.max(jnp.where(fresh_ok, fresh_scores, -jnp.inf), axis=-1),
    )
    suffix_weights = jnp.where(suffix_ok, jnp.exp(suffix_scores - own_high[..., None]), 0.0)
    fresh_weights = jnp.where(fresh_ok, jnp.exp(fresh_scores - own_high[..., None]), 0.0)
    own_sum = jnp.sum(suffix_weights, axis=-1) + jnp.sum(fresh_weights, axis=-1)
    own_numerator = jnp.einsum(
        "rtgjk,rkgd->rtgjd",
        suffix_weights.astype(jnp.bfloat16),
        own_values,
        preferred_element_type=jnp.float32,
    )
    own_numerator = own_numerator + jnp.einsum(
        "rtgjk,rkgd->rtgjd",
        fresh_weights.astype(jnp.bfloat16),
        new_values_split,
        preferred_element_type=jnp.float32,
    )
    own_out = (own_numerator / own_sum[..., None]).reshape(row_count, step_count, -1, HD)
    own_lse = (own_high + jnp.log(own_sum)).reshape(row_count, step_count, -1)
    return (own_out, own_lse)


def shards(
    queries,
    new_keys,
    new_values,
    suffix_keys,
    suffix_values,
    suffix_len,
    prompt_keys,
    prompt_values,
    parent,
    prompt_owner,
    prompt_node,
):
    head_queries, head_keys, head_values = (
        lax.all_to_all(queries, "kv", split_axis=2, concat_axis=0, tiled=True),
        lax.all_to_all(new_keys, "kv", split_axis=2, concat_axis=0, tiled=True),
        lax.all_to_all(new_values, "kv", split_axis=2, concat_axis=0, tiled=True),
    )
    row_count, step_count, feature_width = head_queries.shape
    kv_local = head_keys.shape[2] // HD
    head_count = feature_width // HD
    devices_req = lax.axis_size("req")
    capacity = max(2, 2 * row_count // devices_req)
    slot_count = devices_req * capacity
    ancestors = ancestry(parent[None, :])[0]
    pool_keys = prompt_keys.reshape(-1, prompt_keys.shape[2])
    pool_values = prompt_values.reshape(-1, prompt_values.shape[2])
    dest_hits = (prompt_owner[:, None] == jnp.arange(devices_req, dtype=jnp.int32)[None, :]).astype(
        jnp.int32
    )
    before = jnp.cumsum(dest_hits, axis=0) - dest_hits
    rank_in = jnp.sum(before * dest_hits, axis=1)
    slot_of = prompt_owner * capacity + rank_in
    placing = slot_of[:, None] == jnp.arange(slot_count, dtype=jnp.int32)[None, :]
    send_queries = jnp.einsum(
        "rs,rf->sf",
        placing.astype(jnp.bfloat16),
        head_queries.reshape(row_count, step_count * feature_width),
        preferred_element_type=jnp.float32,
    ).astype(jnp.bfloat16)
    send_queries = send_queries.reshape(devices_req, capacity, step_count, feature_width)
    send_nodes = jnp.sum(jnp.where(placing, prompt_node[:, None], 0), axis=0)
    send_nodes = send_nodes.reshape(devices_req, capacity)
    own_out, own_lse = own_partial(
        head_queries, suffix_keys, suffix_values, head_keys, head_values, suffix_len, kv_local
    )
    place_float = placing.astype(jnp.float32)
    send_out = jnp.einsum(
        "rs,rf->sf", place_float, own_out.reshape(row_count, -1), precision=lax.Precision.HIGHEST
    )
    send_out = send_out.reshape(devices_req, capacity, step_count, head_count, HD)
    send_lse = jnp.einsum(
        "rs,rf->sf", place_float, own_lse.reshape(row_count, -1), precision=lax.Precision.HIGHEST
    )
    send_lse = send_lse.reshape(devices_req, capacity, step_count, head_count)
    got_queries, got_nodes = (
        lax.all_to_all(send_queries, "req", split_axis=0, concat_axis=0, tiled=True),
        lax.all_to_all(send_nodes, "req", split_axis=0, concat_axis=0, tiled=True),
    )
    got_out, got_lse = (
        lax.all_to_all(send_out, "req", split_axis=0, concat_axis=0, tiled=True),
        lax.all_to_all(send_lse, "req", split_axis=0, concat_axis=0, tiled=True),
    )
    part_out, part_lse = prompt_partial(
        got_queries, got_nodes, pool_keys, pool_values, ancestors, kv_local
    )
    finished = merge_parts(part_out, part_lse, got_out, got_lse).astype(jnp.bfloat16)
    finished = finished.reshape(devices_req, capacity, step_count, feature_width)
    returned = lax.all_to_all(finished, "req", split_axis=0, concat_axis=0, tiled=True)
    attended = jnp.take(returned.reshape(slot_count, step_count, feature_width), slot_of, axis=0)
    return lax.all_to_all(attended, "kv", split_axis=0, concat_axis=2, tiled=True)


def solution(mesh):
    in_specs = (
        P(("req", "kv"), None, None),
        P(("req", "kv"), None, None),
        P(("req", "kv"), None, None),
        P("req", None, "kv"),
        P("req", None, "kv"),
        P("req"),
        P("req", None, "kv"),
        P("req", None, "kv"),
        P("req"),
        P("req"),
        P("req"),
    )
    out_specs = P(("req", "kv"), None, None)
    return jax.shard_map(shards, mesh=mesh, in_specs=in_specs, out_specs=out_specs, check_vma=False)
```

profile of v0, /device:TPU:1, one launch (start us, length us, event | category | flops | bytes accessed | tf_op | source)
XLA Modules:
  0.0 536.7 jit_solution(16200850617645870847)
XLA Ops:
  0.0 1.1 copy.330
  1.1 1.1 reshape.828
  2.2 10.1 %all-to-all-start.3 = ((bf16[8,2,1024]{2,1,0:T(2,128)(2,1)}), bf16[8,2,1024]{2,1,0:T(2,128)(2,1)S(1)}, u32[]{:S(2)}, u32[]{:S(2)}) async-start(bf16[8,2,1024]{2,1,0:T(2,128)(2,1)} %reshape.828), calls=%async_computation.3 | async-start | bytes 65536 | tf_op jit(solution)/shard_map/all_to_all | solution.py:138
  14.0 1.2 compare_and_fusion
  16.0 8.4 %copy.304 = bf16[2,8,8192]{1,0,2:T(2,128)(2,1)} copy(bf16[2,8,8192]{2,1,0:T(8,128)(2,1)} %param.11) | data formatting | bytes 524288 | tf_op args[0]
  24.3 6.4 %reshape.826 = bf16[8,2,8192]{2,1,0:T(2,128)(2,1)} reshape(bf16[8192,2,8]{2,1,0:T(2,128)(2,1)} %bitcast.410) | data formatting | bytes 524288
  30.8 4.8 all-to-all-start.1
  36.7 1.1 reshape.830
  38.8 3.3 all-to-all-done.1
  42.1 14.1 %all-to-all-start = ((s32[64,1,2]{2,1,0:T(1,128)}), s32[64,1,2]{2,1,0:T(1,128)S(1)}, u32[]{:S(2)}, u32[]{:S(2)}) async-start(s32[64,1,2]{2,1,0:T(1,128)} %bitcast), calls=%async_computation | async-start | bytes 65536 | tf_op jit(solution)/shard_map/all_to_all | solution.py:180
  56.2 5.9 %reshape.827 = bf16[8192,2,8]{2,1,0:T(2,128)(2,1)} reshape(bf16[8,2,8192]{2,1,0:T(2,128)(2,1)S(1)} %all-to-all-done.1) | data formatting | bytes 524288
  62.2 8.9 %copy.305 = bf16[2,8,8,1024]{3,1,0,2:T(8,128)(2,1)S(1)} copy(bf16[2,8,8,1024]{1,0,3,2:T(2,128)(2,1)} %bitcast.409) | data formatting | bytes 524288 | tf_op jit(solution)/shard_map/all_to_all | solution.py:137
  71.1 1.3 select_reduce_fusion.8
  74.1 4.6 all-to-all-start.5
  80.2 3.2 all-to-all-done.5
  83.4 14.8 %all-to-all-start.4 = ((f32[64,1,128]{2,1,0:T(1,128)}), f32[64,1,128]{2,1,0:T(1,128)S(1)}, u32[]{:S(2)}, u32[]{:S(2)}) async-start(f32[64,1,128]{2,1,0:T(1,128)} %reshape.832), calls=%async_computation.4 | async-start | bytes 65536 | tf_op jit(solution)/shard_map/all_to_all | solution.py:184
  99.1 2.8 copy.402
  101.8 9.5 %all-to-all-done.4 = f32[64,1,128]{2,1,0:T(1,128)S(1)} async-done(((f32[64,1,128]{2,1,0:T(1,128)}), f32[64,1,128]{2,1,0:T(1,128)S(1)}, u32[]{:S(2)}, u32[]{:S(2)}) %all-to-all-start.4) | async-done | bytes 32800 | tf_op jit(solution)/shard_map/all_to_all | solution.py:184
  112.0 5.2 all-to-all-start.2
  117.2 1.4 reshape.831
  118.6 1.2 copy.355
  120.1 2.0 fusion.20
  122.2 1.1 reshape_reshape.2
  123.4 1.9 fusion.53
  125.3 4.4 copy.358
  129.7 78.3 %all-to-all-done.2 = bf16[64,2,8,1024]{3,2,1,0:T(8,128)(2,1)S(1)} async-done(((bf16[64,2,8,1024]{3,2,1,0:T(8,128)(2,1)}), bf16[64,2,8,1024]{3,2,1,0:T(8,128)(2,1)S(1)}, u32[]{:S(2)}, u32[]{:S(2)}) %all-to-all-start.2) | async-done | bytes 2097184 | tf_op jit(solution)/shard_map/all_to_all | solution.py:179
  208.1 14.6 %all-to-all-start.6 = ((f32[64,2,8,8,128]{4,3,2,1,0:T(8,128)}), f32[64,2,8,8,128]{4,3,2,1,0:T(8,128)}, u32[]{:S(2)}, u32[]{:S(2)}) async-start(f32[64,2,8,8,128]{4,3,2,1,0:T(8,128)} %copy.358), calls=%async_computation.6 | async-start | bytes 8388608 | tf_op jit(solution)/shard_map/all_to_all | solution.py:183
  229.4 1.0 fusion.36
  230.5 1.3 fusion.34
  233.4 1.1 copy.335
  234.5 1.1 copy.353
  235.5 1.0 copy.359
  236.6 1.7 fusion.10
  238.3 1.1 copy_dynamic-update-slice_fusion.7
  239.4 1.7 fusion.11
  241.1 1.1 copy_dynamic-update-slice_fusion.6
  242.6 1.2 copy_dynamic-update-slice_fusion.5
  244.2 1.1 copy_dynamic-update-slice_fusion.4
  245.7 1.2 copy_dynamic-update-slice_fusion.3
  247.3 1.2 copy_dynamic-update-slice_fusion.2
  248.8 1.1 copy_dynamic-update-slice_fusion.1
  250.4 1.1 copy_dynamic-update-slice_fusion
  251.5 153.0 %all-to-all-done.6 = f32[64,2,8,8,128]{4,3,2,1,0:T(8,128)} async-done(((f32[64,2,8,8,128]{4,3,2,1,0:T(8,128)}), f32[64,2,8,8,128]{4,3,2,1,0:T(8,128)}, u32[]{:S(2)}, u32[]{:S(2)}) %all-to-all-start.6) | async-done | bytes 4194336 | tf_op jit(solution)/shard_map/all_to_all | solution.py:183
  404.5 7.5 %divide_convert_fusion = bf16[64,2,8,8,128]{4,3,2,1,0:T(8,128)(2,1)S(1)} fusion(f32[64,2,8,8,128]{4,3,2,1,0:T(8,128)} %all-to-all-done.6, f32[64,2,8,8,128]{4,3,2,1,0:T(8,128)} %copy_dynamic-update-slice_fusion, f32[64,2,8,8]{3,2,1,0:T(8,128)} %copy.359, f32[64,2,8,8]{3,2,1,0:T(8,128)S(1)} %copy-done.12, f32[64,2,8,8]{3,2,1,0:T(8,128)S(1)} %copy-done.11), kind=kLoop, calls=%fused_computation.2 | loop fusion | flops 5242880 | bytes 10584064 | tf_op jit(solution)/shard_map/convert_element_type | solution.py:189
  412.0 2.3 reshape.780
  414.4 13.3 %all-to-all-start.7 = ((bf16[64,2,8,1024]{3,2,1,0:T(8,128)(2,1)}), bf16[64,2,8,1024]{3,2,1,0:T(8,128)(2,1)S(1)}, u32[]{:S(2)}, u32[]{:S(2)}) async-start(bf16[64,2,8,1024]{3,2,1,0:T(8,128)(2,1)} %reshape.780), calls=%async_computation.7 | async-start | bytes 4194304 | tf_op jit(solution)/shard_map/all_to_all | solution.py:191
  427.7 91.7 %all-to-all-done.7 = bf16[64,2,8,1024]{3,2,1,0:T(8,128)(2,1)S(1)} async-done(((bf16[64,2,8,1024]{3,2,1,0:T(8,128)(2,1)}), bf16[64,2,8,1024]{3,2,1,0:T(8,128)(2,1)S(1)}, u32[]{:S(2)}, u32[]{:S(2)}) %all-to-all-start.7) | async-done | bytes 2097184 | tf_op jit(solution)/shard_map/all_to_all | solution.py:191
  520.1 15.9 %all_to_all.92 = bf16[16,8,1024]{2,1,0:T(8,128)(2,1)S(1)} all-to-all(bf16[16,8,1024]{2,1,0:T(8,128)(2,1)S(1)} %broadcast_select_fusion), channel_id=1, replica_groups=mesh['req'=64,'kv'=8] {'kv'}, dimensions={0} | all-to-all | bytes 524288 | tf_op jit(solution)/shard_map/all_to_all | solution.py:193
  (129 shorter events, 21.3 us)
Async XLA Ops:
  0.0 119.8 %copy-start = (bf16[16,64,128]{2,1,0:T(8,128)(2,1)S(1)}, bf16[16,64,128]{2,1,0:T(8,128)(2,1)}, u32[]{:S(2)}) copy-start(bf16[16,64,128]{2,1,0:T(8,128)(2,1)} %param.15) | copy-start | bytes 786436
  2.2 28.5 %all-to-all-start.3 = ((bf16[8,2,1024]{2,1,0:T(2,128)(2,1)}), bf16[8,2,1024]{2,1,0:T(2,128)(2,1)S(1)}, u32[]{:S(2)}, u32[]{:S(2)}) async-start(bf16[8,2,1024]{2,1,0:T(2,128)(2,1)} %reshape.828), calls=%async_computation.3 | async-start | bytes 65536 | tf_op jit(solution)/shard_map/all_to_all | solution.py:138
  15.9 20.4 %copy-start.16 = (bf16[2,8,1024]{2,1,0:T(8,128)(2,1)S(1)}, bf16[2,8,1024]{2,1,0:T(8,128)(2,1)}, u32[]{:S(2)}) copy-start(bf16[2,8,1024]{2,1,0:T(8,128)(2,1)} %param.13) | copy-start | bytes 98308
  16.0 21.9 %copy-start.18 = (s32[16]{0:T(128)S(1)}, s32[16]{0:T(128)}, u32[]{:S(2)}) copy-start(s32[16]{0:T(128)} %param.16) | copy-start | bytes 196
  30.8 11.3 %all-to-all-start.1 = ((bf16[8,2,8192]{2,1,0:T(2,128)(2,1)}), bf16[8,2,8192]{2,1,0:T(2,128)(2,1)S(1)}, u32[]{:S(2)}, u32[]{:S(2)}) async-start(bf16[8,2,8192]{2,1,0:T(2,128)(2,1)} %reshape.826), calls=%async_computation.1 | async-start | bytes 524288 | tf_op jit(solution)/shard_map/all_to_all | solution.py:137
  42.1 32.0 %all-to-all-start = ((s32[64,1,2]{2,1,0:T(1,128)}), s32[64,1,2]{2,1,0:T(1,128)S(1)}, u32[]{:S(2)}, u32[]{:S(2)}) async-start(s32[64,1,2]{2,1,0:T(1,128)} %bitcast), calls=%async_computation | async-start | bytes 65536 | tf_op jit(solution)/shard_map/all_to_all | solution.py:180
  56.2 16.1 %copy-start.13 = (bf16[16,64,128]{2,1,0:T(8,128)(2,1)S(1)}, bf16[16,64,128]{2,1,0:T(8,128)(2,1)}, u32[]{:S(2)}) copy-start(bf16[16,64,128]{2,1,0:T(8,128)(2,1)} %param.14) | copy-start | bytes 786436
  74.1 9.3 %all-to-all-start.5 = ((bf16[8,2,1024]{2,1,0:T(2,128)(2,1)}), bf16[8,2,1024]{2,1,0:T(2,128)(2,1)S(1)}, u32[]{:S(2)}, u32[]{:S(2)}) async-start(bf16[8,2,1024]{2,1,0:T(2,128)(2,1)} %reshape.830), calls=%async_computation.5 | async-start | bytes 65536 | tf_op jit(solution)/shard_map/all_to_all | solution.py:139
  83.4 28.0 %all-to-all-start.4 = ((f32[64,1,128]{2,1,0:T(1,128)}), f32[64,1,128]{2,1,0:T(1,128)S(1)}, u32[]{:S(2)}, u32[]{:S(2)}) async-start(f32[64,1,128]{2,1,0:T(1,128)} %reshape.832), calls=%async_computation.4 | async-start | bytes 65536 | tf_op jit(solution)/shard_map/all_to_all | solution.py:184
  111.4 0.6 copy-start.14
  112.0 96.1 %all-to-all-start.2 = ((bf16[64,2,8,1024]{3,2,1,0:T(8,128)(2,1)}), bf16[64,2,8,1024]{3,2,1,0:T(8,128)(2,1)S(1)}, u32[]{:S(2)}, u32[]{:S(2)}) async-start(bf16[64,2,8,1024]{3,2,1,0:T(8,128)(2,1)} %bitcast.413), calls=%async_computation.2 | async-start | bytes 4194304 | tf_op jit(solution)/shard_map/all_to_all | solution.py:179
  129.7 92.9 %copy-start.20 = (s32[2]{0:T(128)S(1)}, s32[2]{0:T(128)}, u32[]{:S(2)}) copy-start(s32[2]{0:T(128)} %param.19) | copy-start | bytes 28
  129.7 95.1 %copy-start.15 = (f32[64,1,128]{2,1,0:T(1,128)S(1)}, f32[64,1,128]{2,1,0:T(1,128)}, u32[]{:S(2)}) copy-start(f32[64,1,128]{2,1,0:T(1,128)} %copy-done.14) | copy-start | bytes 98308
  208.1 196.4 %all-to-all-start.6 = ((f32[64,2,8,8,128]{4,3,2,1,0:T(8,128)}), f32[64,2,8,8,128]{4,3,2,1,0:T(8,128)}, u32[]{:S(2)}, u32[]{:S(2)}) async-start(f32[64,2,8,8,128]{4,3,2,1,0:T(8,128)} %copy.358), calls=%async_computation.6 | async-start | bytes 8388608 | tf_op jit(solution)/shard_map/all_to_all | solution.py:183
  226.1 1.0 copy-start.10
  227.4 1.9 copy-start.6
  228.7 1.8 copy-start.2
  229.0 1.5 copy-start.4
  229.4 1.1 copy-start.8
  230.4 1.4 copy-start.7
  230.5 6.1 %copy-start.19 = (bf16[2,128,128]{2,1,0:T(8,128)(2,1)S(1)}, bf16[2,128,128]{2,1,0:T(8,128)(2,1)}, u32[]{:S(2)}) copy-start(bf16[2,128,128]{2,1,0:T(8,128)(2,1)} %param.18) | copy-start | bytes 196612
  236.6 5.7 %copy-start.5 = (f32[128,1,8,2,128]{0,4,3,2,1:T(8,128)S(1)}, f32[128,1,8,2,128]{0,4,3,2,1:T(8,128)}, u32[]{:S(2)}) copy-start(f32[128,1,8,2,128]{0,4,3,2,1:T(8,128)} %copy-done.4) | copy-start | bytes 3145732
  239.4 4.4 copy-start.3
  246.9 3.1 copy-start.9
  248.4 156.1 %copy-start.11 = (f32[64,2,8,8]{3,2,1,0:T(8,128)S(1)}, f32[64,2,8,8]{3,2,1,0:T(8,128)}, u32[]{:S(2)}) copy-start(f32[64,2,8,8]{3,2,1,0:T(8,128)} %copy.335) | copy-start | bytes 98308
  248.4 156.1 %copy-start.12 = (f32[64,2,8,8]{3,2,1,0:T(8,128)S(1)}, f32[64,2,8,8]{3,2,1,0:T(8,128)}, u32[]{:S(2)}) copy-start(f32[64,2,8,8]{3,2,1,0:T(8,128)} %copy.353) | copy-start | bytes 98308
  412.0 108.0 %copy-start.17 = (pred[16]{0:T(512)(128)(4,1)S(1)}, pred[16]{0:T(512)(128)(4,1)}, u32[]{:S(2)}) copy-start(pred[16]{0:T(512)(128)(4,1)} %get-tuple-element.21) | copy-start | bytes 52
  412.0 124.7 %copy-start.1 = (bf16[16,64,128]{2,1,0:T(8,128)(2,1)S(1)}, bf16[16,64,128]{2,1,0:T(8,128)(2,1)}, u32[]{:S(2)}) copy-start(bf16[16,64,128]{2,1,0:T(8,128)(2,1)} %param.15) | copy-start | bytes 786436
  414.4 105.1 %all-to-all-start.7 = ((bf16[64,2,8,1024]{3,2,1,0:T(8,128)(2,1)}), bf16[64,2,8,1024]{3,2,1,0:T(8,128)(2,1)S(1)}, u32[]{:S(2)}, u32[]{:S(2)}) async-start(bf16[64,2,8,1024]{3,2,1,0:T(8,128)(2,1)} %reshape.780), calls=%async_computation.7 | async-start | bytes 4194304 | tf_op jit(solution)/shard_map/all_to_all | solution.py:191
where the time goes:
time: 539 us; the launch traced here: 537 us
  waiting for transfers between devices  339 us (63%)
  starting transfers between devices  81.5 us (15%)
  local copies, waits for them, and re-layouts  68.1 us (13%)
  blocking collectives  15.9 us (3%)
  matrix products  15.8 us (3%)
  other arithmetic  15.7 us (3%)
    all_to_all x1, waiting for transfers between devices, shards(): lax.all_to_all(send_out, 'req', split_axis=0, concat_axis=0, tiled=True)  153 us
    all_to_all x1, waiting for transfers between devices, shards(): lax.all_to_all(finished, 'req', split_axis=0, concat_axis=0, tiled=True)  91.7 us
    all_to_all x1, waiting for transfers between devices, shards(): lax.all_to_all(send_queries, 'req', split_axis=0, concat_axis=0, tiled=True)  78.3 us
    unnamed x71, local copies, waits for them, and re-layouts  40 us
    all_to_all x1, blocking collectives, shards(): lax.all_to_all(attended, 'kv', split_axis=0, concat_axis=2, tiled=True)  15.9 us
    all_to_all x1, starting transfers between devices, shards(): lax.all_to_all(send_lse, 'req', split_axis=0, concat_axis=0, tiled=True)  14.8 us
    all_to_all x1, starting transfers between devices, shards(): lax.all_to_all(send_out, 'req', split_axis=0, concat_axis=0, tiled=True)  14.6 us
    all_to_all x1, starting transfers between devices, shards(): lax.all_to_all(send_nodes, 'req', split_axis=0, concat_axis=0, tiled=True)  14.1 us
  transfers between devices with their start and end apart: 8, of which 6 were waited for; matrix products, arithmetic and copies ran while one was open for 16% of the time, Pallas kernels for 0%

commit v1 on v0

v1 whole, which is shorter than its diff:
```python
import functools
import math

import jax
import jax.numpy as jnp
from jax import lax
from jax.experimental import pallas as pl
from jax.experimental.pallas import tpu as pltpu
from jax.sharding import PartitionSpec as P

MESH = pl.DeviceIdType.MESH
BF16, F32, I32 = jnp.bfloat16, jnp.float32, jnp.int32

HD = 128
BLK = 128
STEPS = 8
GROUP = 8
SUF = 64
NX = 4
PIECES = 2
FLAG = 16
LOW = -1e30
EXPO = math.log2(math.e) / math.sqrt(HD)

NN = (((1,), (0,)), ((), ()))
NT = (((1,), (1,)), ((), ()))


def dot(a, b, dims=NN):
    return lax.dot_general(a, b, dims, preferred_element_type=F32)


def ring_tree(half):
    return {d: d - 1 for d in range(1, half + 1)}


LAGS = (2, 4)


def kernel(
    nz, nkv,
    q_hbm, nk_hbm, nv_hbm, sk_hbm, sv_hbm, pk_hbm, pv_hbm, len_hbm, par_hbm, owner_hbm, node_hbm,
    out_ref,
    k_all, v_nat, v_all, q_all, nk, nv, sk, sv,
    meta, meta_s, len_s, par_s, owner_s, node_s,
    w_all, st_p, st_in, st_own, own_num, fac, ret, ret_in, fin_out, fin,
    loc_sem, meta_sem, ring_ss, ring_rs, a2a_ss, a2a_rs, x_ss, x_rs, m_ss, m_rs, st_ss, st_rs,
    ret_ss, ret_rs, fin_ss, fin_rs,
):
    r, k = lax.axis_index("req"), lax.axis_index("kv")
    x, z = r // nz, r % nz
    half = nz // 2
    hdp = HD // PIECES
    rows2 = 2 * STEPS

    def at_z(d):
        return (x * nz + (z + d + nz) % nz, k)

    def at_x(d):
        return (((x + d) % NX) * nz + z, k)

    def at_k(o):
        return (r, (k + o) % nkv)

    def remote(src, dst, ss, rs, dev):
        return pltpu.make_async_remote_copy(
            src_ref=src, dst_ref=dst, send_sem=ss, recv_sem=rs, device_id=dev, device_id_type=MESH
        )

    local = [
        pltpu.make_async_copy(pk_hbm, k_all.at[z, 0 : 2 * BLK], loc_sem.at[0]),
        pltpu.make_async_copy(pv_hbm, v_nat, loc_sem.at[1]),
        pltpu.make_async_copy(par_hbm, par_s, loc_sem.at[2]),
        pltpu.make_async_copy(owner_hbm, owner_s, loc_sem.at[3]),
        pltpu.make_async_copy(node_hbm, node_s, loc_sem.at[4]),
        pltpu.make_async_copy(len_hbm, len_s, loc_sem.at[5]),
        pltpu.make_async_copy(
            q_hbm.at[:, pl.ds(pl.multiple_of(k * (GROUP * HD), HD), GROUP * HD)], q_all.at[x, k], loc_sem.at[6]
        ),
        pltpu.make_async_copy(nk_hbm.at[:, pl.ds(pl.multiple_of(k * HD, HD), HD)], nk.at[k], loc_sem.at[7]),
        pltpu.make_async_copy(nv_hbm.at[:, pl.ds(pl.multiple_of(k * HD, HD), HD)], nv.at[k], loc_sem.at[8]),
        pltpu.make_async_copy(sk_hbm, sk, loc_sem.at[9]),
        pltpu.make_async_copy(sv_hbm, sv, loc_sem.at[10]),
    ]
    for c in local:
        c.start()

    barrier = pltpu.get_barrier_semaphore()
    peers = [at_z(1), at_z(-1)] + [at_x(d) for d in range(1, NX)] + [at_k(o) for o in range(1, nkv)]
    for dev in peers:
        pl.semaphore_signal(barrier, inc=1, device_id=dev, device_id_type=MESH)
    local[2].wait()
    flag = jnp.where(par_s[1] == 0, 0.0, LOW).astype(F32)
    k_all[z, 2 * BLK : 2 * BLK + FLAG] = jnp.full((FLAG, HD), flag, F32).astype(BF16)
    local[0].wait()
    pl.semaphore_wait(barrier, len(peers))

    tree = ring_tree(half)
    stage = {0: 0}
    for d in range(1, half + 1):
        stage[d] = stage[tree[d]] + 1
    depth = max(stage.values())
    kc = BLK

    def k_chunk(lo, hi):
        return lambda b, part: k_all.at[b, lo:hi]

    def v_chunk(p):
        def at(b, part):
            if part is None:
                return v_all[p].at[b]
            return v_all[p].at[b, part * (hdp // 2) : (part + 1) * (hdp // 2)]

        return at

    chunks = [(0, k_chunk(0, kc), 0), (1, k_chunk(kc, 2 * BLK + FLAG), 0)]
    chunks += [(2 + p, v_chunk(p), LAGS[p]) for p in range(PIECES)]

    def carried(c, dirn, d):
        if d < half:
            return True, None
        if c < 2:
            return c == dirn, None
        return True, dirn

    def hand_on(c, at, d, dirn):
        sign = 1 - 2 * dirn
        block = (z - sign * d + nz) % nz
        for e in sorted((e for e in tree if tree[e] == d), reverse=True):
            ok, part = carried(c, dirn, e)
            if ok:
                ref = at(block, part)
                remote(ref, ref, ring_ss.at[dirn, c, e], ring_rs.at[dirn, c, e], at_z(sign * (e - d))).start()

    def arrive(c, at, d, dirn):
        sign = 1 - 2 * dirn
        ok, part = carried(c, dirn, d)
        if ok:
            ref = at((z - sign * d + nz) % nz, part)
            remote(ref, ref, ring_ss.at[dirn, c, d], ring_rs.at[dirn, c, d], at_z(sign)).wait_recv()

    def slot(t):
        for c, at, lag in chunks:
            for d in range(half + 1):
                if lag + stage[d] != t:
                    continue
                for dirn in (0, 1):
                    if d > 0:
                        arrive(c, at, d, dirn)
                    hand_on(c, at, d, dirn)

    def drain():
        for c, at, lag in chunks:
            for d in range(1, half + 1):
                for dirn in (0, 1):
                    ok, part = carried(c, dirn, d)
                    if ok:
                        ref = at((z - (1 - 2 * dirn) * tree[d] + nz) % nz, part)
                        remote(ref, ref, ring_ss.at[dirn, c, d], ring_rs.at[dirn, c, d], at_z(1)).wait_send()

    def a2a(i, o, got=False):
        to = (k + o) % nkv
        frm = (k + nkv - o) % nkv
        wide = pl.ds(pl.multiple_of(to * (GROUP * HD), HD), GROUP * HD)
        thin = pl.ds(pl.multiple_of(to * HD, HD), HD)
        src = (q_hbm.at[:, wide], nk_hbm.at[:, thin], nv_hbm.at[:, thin])[i]
        dst = (q_all.at[x], nk, nv)[i]
        if got:
            src, dst = dst.at[frm], dst.at[frm]
        else:
            dst = dst.at[k]
        return remote(src, dst, a2a_ss.at[i, o], a2a_rs.at[i, o], at_k(o))

    slot(0)
    for i in range(3):
        for o in range(1, nkv):
            a2a(i, o).start()

    local[3].wait()
    local[4].wait()
    local[5].wait()
    lane = lax.broadcasted_iota(I32, (1, HD), 1)
    own_z = own_x = nodes = jnp.zeros((1, HD), I32)
    for i in range(2 * nkv):
        own_z = jnp.where(lane == i, owner_s[i] % nz, own_z)
        own_x = jnp.where(lane == i, owner_s[i] // nz, own_x)
        nodes = jnp.where(lane == i, node_s[i], nodes)
    pad = jnp.zeros((5, HD), I32)
    meta[x] = jnp.concatenate([own_z, own_x, nodes, pad], axis=0)
    for d in range(1, NX):
        remote(meta.at[x], meta.at[x], m_ss.at[d], m_rs.at[d], at_x(d)).start()

    local[1].wait()
    v_t = v_nat[...].astype(F32).T.astype(BF16)
    for p in range(PIECES):
        v_all[p][z] = v_t[p * hdp : (p + 1) * hdp]

    first = (lane // STEPS) % 2 == 0

    def both(a, b):
        return jnp.where(first, a, b)

    def pair_queries(src, p):
        slab = q_all[src, p]
        return jnp.concatenate([slab[:, j * HD : (j + 1) * HD] for j in range(GROUP)], axis=0)

    def send_queries():
        for o in range(1, nkv):
            a2a(0, o, True).wait_recv()
        local[6].wait()
        for d in (1, 3, 2):
            remote(q_all.at[x], q_all.at[x], x_ss.at[d], x_rs.at[d], at_x(d)).start()

    def await_queries(d):
        src = (x + d) % NX
        remote(q_all.at[src], q_all.at[src], x_ss.at[NX - d], x_rs.at[NX - d], at_x(d)).wait_recv()

    def await_meta():
        for d in range(1, NX):
            src = (x + d) % NX
            remote(meta.at[src], meta.at[src], m_ss.at[NX - d], m_rs.at[NX - d], at_x(d)).wait_recv()
        c = pltpu.make_async_copy(meta, meta_s, meta_sem.at[0])
        c.start()
        c.wait()

    def await_own():
        for o in range(1, nkv):
            a2a(1, o, True).wait_recv()
            a2a(2, o, True).wait_recv()
        for i in (7, 8, 9, 10):
            local[i].wait()

    def own_pair(p):
        queries = pair_queries(x, p)
        len_a, len_b = len_s[2 * p], len_s[2 * p + 1]
        s_suf = both(dot(sk[2 * p], queries, NT), dot(sk[2 * p + 1], queries, NT))
        s_new = dot(nk[p], queries, NT)
        pos = lax.broadcasted_iota(I32, (SUF, HD), 0)
        s_suf = jnp.where(pos < both(len_a, len_b), s_suf, LOW)
        row = lax.broadcasted_iota(I32, (rows2, HD), 0)
        col = lax.broadcasted_iota(I32, (rows2, HD), 1)
        seen = (row // STEPS == (col // STEPS) % 2) & (row % STEPS <= col % STEPS)
        s_new = jnp.where(seen, s_new, LOW)
        peak = jnp.maximum(jnp.max(s_suf, axis=0, keepdims=True), jnp.max(s_new, axis=0, keepdims=True))
        w_suf = jnp.exp2((s_suf - peak) * EXPO)
        w_new = jnp.exp2((s_new - peak) * EXPO)
        total = jnp.sum(w_suf, axis=0, keepdims=True) + jnp.sum(w_new, axis=0, keepdims=True)
        w_suf, w_new = w_suf.astype(BF16), w_new.astype(BF16)
        va = sv[2 * p].astype(F32).T.astype(BF16)
        vb = sv[2 * p + 1].astype(F32).T.astype(BF16)
        vn = nv[p].astype(F32).T.astype(BF16)
        own_num[p] = both(dot(va, w_suf), dot(vb, w_suf)) + dot(vn, w_new)
        st_own[0, p : p + 1] = peak
        st_own[1, p : p + 1] = total

    def prompt_weights(d, p):
        src = (x + d) % NX
        a, b = 2 * p, 2 * p + 1
        queries = pair_queries(src, p)
        ka, kb = meta_s[src, 0, a], meta_s[src, 0, b]
        node_a, node_b = meta_s[src, 2, a], meta_s[src, 2, b]
        s = both(dot(k_all[ka, 0 : 2 * BLK], queries, NT), dot(k_all[kb, 0 : 2 * BLK], queries, NT))
        flag_a = k_all[ka, 2 * BLK : 2 * BLK + FLAG].astype(F32)[0:1]
        flag_b = k_all[kb, 2 * BLK : 2 * BLK + FLAG].astype(F32)[0:1]
        nodes_ab = both(node_a, node_b)
        s0 = s[0:BLK] + jnp.where(nodes_ab == 1, both(flag_a, flag_b), 0.0)
        s1 = s[BLK:] + jnp.where(nodes_ab == 1, 0.0, LOW)
        peak = jnp.max(jnp.maximum(s0, s1), axis=0, keepdims=True)
        w0 = jnp.exp2((s0 - peak) * EXPO)
        w1 = jnp.exp2((s1 - peak) * EXPO)
        st_p[d, 0, p : p + 1] = peak
        st_p[d, 1, p : p + 1] = jnp.sum(w0 + w1, axis=0, keepdims=True)
        w_all[d, p, 0:BLK] = w0.astype(BF16)
        w_all[d, p, BLK:] = w1.astype(BF16)

    def send_stats(d):
        e = NX - d
        remote(st_p.at[d], st_in.at[e], st_ss.at[d], st_rs.at[e], at_x(d)).start()

    def prompt_values(piece, d, p):
        src = (x + d) % NX
        va = v_all[piece][meta_s[src, 0, 2 * p]]
        vb = v_all[piece][meta_s[src, 0, 2 * p + 1]]
        w = w_all[d, p]
        ret[piece, d, p] = both(dot(va, w), dot(vb, w)).astype(BF16)

    def send_back(piece, d):
        e = NX - d
        remote(
            ret.at[piece, d], ret_in.at[piece, e], ret_ss.at[piece, d], ret_rs.at[piece, e], at_x(d)
        ).start()

    def await_back(piece):
        for e in range(1, NX):
            remote(
                ret_in.at[piece, e], ret_in.at[piece, e], ret_ss.at[piece, e], ret_rs.at[piece, e], at_x(e)
            ).wait_recv()

    def owner_side(p):
        xa, xb = meta_s[x, 1, 2 * p], meta_s[x, 1, 2 * p + 1]
        return both((xa - x + NX) % NX, (xb - x + NX) % NX)

    def factors():
        for e in range(1, NX):
            remote(st_in.at[e], st_in.at[e], st_ss.at[e], st_rs.at[e], at_x(e)).wait_recv()
        for p in range(nkv):
            side = owner_side(p)
            peak, total = st_p[0, 0, p : p + 1], st_p[0, 1, p : p + 1]
            for e in range(1, NX):
                peak = jnp.where(side == e, st_in[e, 0, p : p + 1], peak)
                total = jnp.where(side == e, st_in[e, 1, p : p + 1], total)
            peak_own, total_own = st_own[0, p : p + 1], st_own[1, p : p + 1]
            top = jnp.maximum(peak, peak_own)
            f_p = jnp.exp2((peak - top) * EXPO)
            f_o = jnp.exp2((peak_own - top) * EXPO)
            inv = 1.0 / (f_p * total + f_o * total_own)
            fac[0, p : p + 1] = f_p * inv
            fac[1, p : p + 1] = f_o * inv

    def merge(piece, p):
        side = owner_side(p)
        num = ret[piece, 0, p].astype(F32)
        for e in range(1, NX):
            num = jnp.where(side == e, ret_in[piece, e, p].astype(F32), num)
        own = own_num[p, piece * hdp : (piece + 1) * hdp]
        fin_out[piece, p] = (num * fac[0, p : p + 1] + own * fac[1, p : p + 1]).astype(BF16)

    def send_final(piece):
        for o in range(1, nkv):
            to = (k + o) % nkv
            remote(
                fin_out.at[piece, to], fin.at[piece, k], fin_ss.at[piece, o], fin_rs.at[piece, o], at_k(o)
            ).start()
        fin[piece, k] = fin_out[piece, k]

    scores = [(d, p) for d in (0, 1, 3, 2) for p in range(nkv)]
    before = {t: [] for t in range(1, LAGS[-1] + depth + 1)}

    def plan(t, f, *args):
        before[min(max(t, 1), LAGS[-1] + depth)].append(functools.partial(f, *args))

    plan(2, send_queries)
    plan(3, await_own)
    for p in range(nkv):
        plan(3 + (p * 3) // nkv, own_pair, p)
    plan(min(6, depth + 1), await_meta)
    late = []
    k_done = depth + 1
    v0_done = LAGS[0] + depth + 1
    gap = max(v0_done - k_done, 1)
    for i, (d, p) in enumerate(scores):
        t = k_done + (i * gap) // len(scores)
        if p == 0 and d:
            plan(t, await_queries, d)
        plan(t, prompt_weights, d, p)
        if p == nkv - 1 and d:
            plan(t, send_stats, d)
    values = [(d, p) for d in (2, 1, 3, 0) for p in range(nkv)]
    gap = LAGS[1] - LAGS[0]
    for i, (d, p) in enumerate(values):
        t = v0_done + (i * gap) // len(values)
        plan(t, prompt_values, 0, d, p)
        if p == nkv - 1 and d:
            plan(t, send_back, 0, d)

    for t in range(1, LAGS[-1] + depth + 1):
        for f in before[t]:
            f()
        slot(t)
    for d, p in values:
        prompt_values(1, d, p)
        if p == nkv - 1 and d:
            send_back(1, d)
    factors()
    for piece in range(PIECES):
        await_back(piece)
        for p in range(nkv):
            merge(piece, p)
        send_final(piece)
    for piece in range(PIECES):
        for o in range(1, nkv):
            frm = (k + nkv - o) % nkv
            remote(
                fin.at[piece, frm], fin.at[piece, frm], fin_ss.at[piece, o], fin_rs.at[piece, o], at_k(o)
            ).wait_recv()
    for g in range(nkv):
        rows = jnp.concatenate([fin[piece, g].astype(F32) for piece in range(PIECES)], axis=0)
        rows = rows.T.astype(BF16)
        for j in range(GROUP):
            out_ref[:, (g * GROUP + j) * HD : (g * GROUP + j + 1) * HD] = rows[j * rows2 : (j + 1) * rows2]

    drain()
    for o in range(1, nkv):
        for i in range(3):
            a2a(i, o).wait_send()
        for piece in range(PIECES):
            remote(
                fin_out.at[piece, 0], fin.at[piece, 0], fin_ss.at[piece, o], fin_rs.at[piece, o], at_k(o)
            ).wait_send()
    for d in range(1, NX):
        remote(q_all.at[x], q_all.at[x], x_ss.at[d], x_rs.at[d], at_x(d)).wait_send()
        remote(meta.at[x], meta.at[x], m_ss.at[d], m_rs.at[d], at_x(d)).wait_send()
        remote(st_p.at[d], st_in.at[d], st_ss.at[d], st_rs.at[d], at_x(d)).wait_send()
        for piece in range(PIECES):
            remote(
                ret.at[piece, d], ret_in.at[piece, d], ret_ss.at[piece, d], ret_rs.at[piece, d], at_x(d)
            ).wait_send()


def solution(mesh):
    nz = mesh.shape["req"] // NX
    nkv = mesh.shape["kv"]
    half = nz // 2
    hdp = HD // PIECES
    rows2 = 2 * STEPS

    def shards(q, nk, nv, sk, sv, length, pk, pv, parent, owner, node):
        q = q.reshape(rows2, -1)
        nk = nk.reshape(rows2, -1)
        nv = nv.reshape(rows2, -1)
        pk = pk.reshape(2 * BLK, HD)
        pv = pv.reshape(2 * BLK, HD)
        dma = pltpu.SemaphoreType.DMA
        vmem = pltpu.VMEM
        out = pl.pallas_call(
            functools.partial(kernel, nz, nkv),
            out_shape=jax.ShapeDtypeStruct((rows2, nkv * GROUP * HD), BF16),
            in_specs=[pl.BlockSpec(memory_space=pl.ANY)] * 11,
            out_specs=pl.BlockSpec(memory_space=pltpu.VMEM),
            scratch_shapes=[
                vmem((nz, 2 * BLK + FLAG, HD), BF16),
                vmem((2 * BLK, HD), BF16),
                [vmem((nz, hdp, 2 * BLK), BF16)] * PIECES,
                vmem((NX, nkv, rows2, GROUP * HD), BF16),
                vmem((nkv, rows2, HD), BF16),
                vmem((nkv, rows2, HD), BF16),
                vmem((2 * nkv, SUF, HD), BF16),
                vmem((2 * nkv, SUF, HD), BF16),
                vmem((NX, 8, HD), I32),
                pltpu.SMEM((NX, 8, HD), I32),
                pltpu.SMEM((2 * nkv,), I32),
                pltpu.SMEM((2,), I32),
                pltpu.SMEM((2 * nkv,), I32),
                pltpu.SMEM((2 * nkv,), I32),
                vmem((NX, nkv, 2 * BLK, HD), BF16),
                vmem((NX, 2, nkv, HD), F32),
                vmem((NX, 2, nkv, HD), F32),
                vmem((2, nkv, HD), F32),
                vmem((nkv, HD, HD), F32),
                vmem((2, nkv, HD), F32),
                vmem((PIECES, NX, nkv, hdp, HD), BF16),
                vmem((PIECES, NX, nkv, hdp, HD), BF16),
                vmem((PIECES, nkv, hdp, HD), BF16),
                vmem((PIECES, nkv, hdp, HD), BF16),
                dma((11,)),
                dma((1,)),
                dma((2, 2 + PIECES, half + 1)),
                dma((2, 2 + PIECES, half + 1)),
                dma((3, nkv)),
                dma((3, nkv)),
                dma((NX,)),
                dma((NX,)),
                dma((NX,)),
                dma((NX,)),
                dma((NX,)),
                dma((NX,)),
                dma((PIECES, NX)),
                dma((PIECES, NX)),
                dma((PIECES, nkv)),
                dma((PIECES, nkv)),
            ],
            compiler_params=pltpu.CompilerParams(
                collective_id=0, has_side_effects=True, vmem_limit_bytes=32 * 2**20
            ),
        )(q, nk, nv, sk, sv, pk, pv, length, parent, owner, node)
        return out.reshape(2, STEPS, -1)

    in_specs = (
        P(("req", "kv"), None, None),
        P(("req", "kv"), None, None),
        P(("req", "kv"), None, None),
        P("req", None, "kv"),
        P("req", None, "kv"),
        P("req"),
        P("req", None, "kv"),
        P("req", None, "kv"),
        P("req"),
        P("req"),
        P("req"),
    )
    return jax.shard_map(
        shards, mesh=mesh, in_specs=in_specs, out_specs=P(("req", "kv"), None, None), check_vma=False
    )
```

time: 539 us -> 76.4 us (0.14)
  waiting for transfers between devices: 339 us -> 0 us
  starting transfers between devices: 81.5 us -> 0 us
  Pallas kernels: 0 us -> 68.5 us
  local copies, waits for them, and re-layouts: 68.1 us -> 7.44 us
  blocking collectives: 15.9 us -> 0 us
  matrix products: 15.8 us -> 0 us
  other arithmetic: 15.7 us -> 0 us
    all_to_all x8 -> x0, waiting for transfers between devices: 339 us -> none  [the longest x1 153 us: shards(): lax.all_to_all(send_out, 'req', split_axis=0, concat_axis=0, tiled=True)]
    all_to_all x8 -> x0, starting transfers between devices: 81.5 us -> none  [the longest x1 14.8 us: shards(): lax.all_to_all(send_lse, 'req', split_axis=0, concat_axis=0, tiled=True)]
    pallas_call x0 -> x1, Pallas kernels: none -> 68.5 us  [shards(): pl.pallas_call(functools.partial(kernel, nz, nkv), out_shape=jax.ShapeDty...]
    unnamed x71 -> x23, local copies, waits for them, and re-layouts: 40 us -> 7.44 us
    all_to_all x1 -> x0, blocking collectives: 15.9 us -> none  [shards(): lax.all_to_all(attended, 'kv', split_axis=0, concat_axis=2, tiled=True)]
    dot_general x23 -> x0, matrix products: 15.8 us -> none  [the longest x8 5.68 us: prompt_partial(): jnp.einsum('cgjbw,bwgd->cgjd', weights.astype(jnp.bfloat16), block_values...]
    all_to_all x8 -> x0, local copies, waits for them, and re-layouts: 13.1 us -> none  [the longest x1 8.88 us: shards(): lax.all_to_all(queries, 'kv', split_axis=2, concat_axis=0, tiled=True)]
    convert_element_type x2 -> x0, other arithmetic: 8.21 us -> none  [the longest x1 7.49 us: shards(): merge_parts(part_out, part_lse, got_out, got_lse).astype(jnp.bfloat16)]
  transfers between devices with their start and end apart: 8 -> 0, of which waited for: 6 -> 0; matrix products, arithmetic and copies ran while one was open for 16% -> 0% of each run, Pallas kernels for 0% -> 0%
where the time goes in v1:
time: 76.4 us; the launch traced here: 75.9 us
  Pallas kernels  68.5 us (90%)
  local copies, waits for them, and re-layouts  7.44 us (10%)
    pallas_call x1, Pallas kernels, shards(): pl.pallas_call(functools.partial(kernel, nz, nkv), out_shape=jax.ShapeDty...  68.5 us
    unnamed x23, local copies, waits for them, and re-layouts  7.44 us

profile of v1, /device:TPU:1, one launch (start us, length us, event | category | flops | bytes accessed | tf_op | source)
XLA Modules:
  0.0 75.9 jit_solution(16212329973818593649)
XLA Ops:
  0.0 0.0 copy-start.10
  0.0 0.0 copy-start.7
  0.0 0.0 copy-start.8
  0.0 0.0 copy-start.9
  0.0 0.6 copy-done.10
  0.7 0.0 copy-done.7
  0.7 0.0 copy-done.8
  0.7 0.0 copy-done.9
  0.7 0.0 copy-start
  0.7 0.9 %copy-done = bf16[2,8,8192]{2,1,0:T(8,128)(2,1)S(1)} copy-done((bf16[2,8,8192]{2,1,0:T(8,128)(2,1)S(1)}, bf16[2,8,8192]{2,1,0:T(8,128)(2,1)}, u32[]{:S(2)}) %copy-start) | copy-done | bytes 262168
  1.7 0.0 copy-start.1
  1.7 0.9 %copy-done.1 = bf16[16,64,128]{2,1,0:T(8,128)(2,1)S(1)} copy-done((bf16[16,64,128]{2,1,0:T(8,128)(2,1)S(1)}, bf16[16,64,128]{2,1,0:T(8,128)(2,1)}, u32[]{:S(2)}) %copy-start.1) | copy-done | bytes 262168
  2.6 0.0 copy-start.2
  2.6 0.9 %copy-done.2 = bf16[16,64,128]{2,1,0:T(8,128)(2,1)S(1)} copy-done((bf16[16,64,128]{2,1,0:T(8,128)(2,1)S(1)}, bf16[16,64,128]{2,1,0:T(8,128)(2,1)}, u32[]{:S(2)}) %copy-start.2) | copy-done | bytes 262168
  3.6 0.0 copy-start.3
  3.6 0.8 %copy-done.3 = bf16[2,128,128]{2,1,0:T(8,128)(2,1)S(1)} copy-done((bf16[2,128,128]{2,1,0:T(8,128)(2,1)S(1)}, bf16[2,128,128]{2,1,0:T(8,128)(2,1)}, u32[]{:S(2)}) %copy-start.3) | copy-done | bytes 65560
  4.4 0.0 copy-start.4
  4.4 0.8 %copy-done.4 = bf16[2,128,128]{2,1,0:T(8,128)(2,1)S(1)} copy-done((bf16[2,128,128]{2,1,0:T(8,128)(2,1)S(1)}, bf16[2,128,128]{2,1,0:T(8,128)(2,1)}, u32[]{:S(2)}) %copy-start.4) | copy-done | bytes 65560
  5.2 0.0 copy-start.5
  5.2 0.8 copy-done.5
  6.0 0.0 copy-start.6
  6.0 0.8 copy-done.6
  6.8 68.5 %shard_map.109 = bf16[16,8192]{1,0:T(8,128)(2,1)S(1)} custom-call(bf16[16,8192]{1,0:T(8,128)(2,1)S(1)} %bitcast.7, bf16[16,1024]{1,0:T(8,128)(2,1)S(1)} %bitcast.10, bf16[16,1024]{1,0:T(8,128)(2,1)S(1)} %bitcast.11, bf16[16,64,128]{2,1,0:T(8,128)(2,1)S(1)} %copy-done.1, bf16[16,64,128]{2,1,0:T(8,128)(2,1)S(1)} %copy-done.2, bf16[256,128]{1,0:T(8,128)(2,1)S(1)} %bitcast.8, ...), custom_call_target="tpu_custom_call" | custom-call | tf_op jit(solution)/shard_map/pallas_call | solution.py:425
  75.2 0.7 copy.13
Async XLA Ops:
  0.0 0.7 copy-start.10
  0.0 0.7 copy-start.7
  0.0 0.7 copy-start.8
  0.0 0.7 copy-start.9
  0.7 0.9 %copy-start = (bf16[2,8,8192]{2,1,0:T(8,128)(2,1)S(1)}, bf16[2,8,8192]{2,1,0:T(8,128)(2,1)}, u32[]{:S(2)}) copy-start(bf16[2,8,8192]{2,1,0:T(8,128)(2,1)} %param.11) | copy-start | bytes 786436
  1.7 0.9 %copy-start.1 = (bf16[16,64,128]{2,1,0:T(8,128)(2,1)S(1)}, bf16[16,64,128]{2,1,0:T(8,128)(2,1)}, u32[]{:S(2)}) copy-start(bf16[16,64,128]{2,1,0:T(8,128)(2,1)} %sk_hbm.1) | copy-start | bytes 786436
  2.6 0.9 %copy-start.2 = (bf16[16,64,128]{2,1,0:T(8,128)(2,1)S(1)}, bf16[16,64,128]{2,1,0:T(8,128)(2,1)}, u32[]{:S(2)}) copy-start(bf16[16,64,128]{2,1,0:T(8,128)(2,1)} %sv_hbm.1) | copy-start | bytes 786436
  3.6 0.8 %copy-start.3 = (bf16[2,128,128]{2,1,0:T(8,128)(2,1)S(1)}, bf16[2,128,128]{2,1,0:T(8,128)(2,1)}, u32[]{:S(2)}) copy-start(bf16[2,128,128]{2,1,0:T(8,128)(2,1)} %param.17) | copy-start | bytes 196612
  4.4 0.8 %copy-start.4 = (bf16[2,128,128]{2,1,0:T(8,128)(2,1)S(1)}, bf16[2,128,128]{2,1,0:T(8,128)(2,1)}, u32[]{:S(2)}) copy-start(bf16[2,128,128]{2,1,0:T(8,128)(2,1)} %param.18) | copy-start | bytes 196612
  5.2 0.8 copy-start.5
  6.0 0.8 copy-start.6

commit v2 on v1

v2 whole, which is shorter than its diff:
```python
import functools
import math

import jax
import jax.numpy as jnp
from jax import lax
from jax.experimental import pallas as pl
from jax.experimental.pallas import tpu as pltpu
from jax.sharding import PartitionSpec as P

MESH = pl.DeviceIdType.MESH
BF16, F32, I32 = jnp.bfloat16, jnp.float32, jnp.int32

HD = 128
BLK = 128
STEPS = 8
GROUP = 8
SUF = 64
NX = 4
FLAG = 16
LOW = -1e30
EXPO = math.log2(math.e) / math.sqrt(HD)

NN = (((1,), (0,)), ((), ()))
NT = (((1,), (1,)), ((), ()))


def dot(a, b, dims=NN):
    return lax.dot_general(a, b, dims, preferred_element_type=F32)


def block_tree(half, jumps):
    tree = {d: d - 1 for d in range(1, half + 1)}
    tree.update({d: frm for d, frm in jumps.items() if d <= half})
    stage = {0: 0}
    while len(stage) <= half:
        stage.update({d: stage[frm] + 1 for d, frm in tree.items() if frm in stage})
    return tree, stage


LAGS = (0, 0)
JUMPS = ({8: 6}, {})


def kernel(
    nz, nkv,
    q_hbm, nk_hbm, nv_hbm, sk_hbm, sv_hbm, pk_hbm, pv_hbm, len_hbm, par_hbm, owner_hbm, node_hbm,
    fin,
    k_all, v_nat, v_all, q_all, nk, nv, sk, sv,
    meta, meta_s, len_s, par_s, owner_s, node_s,
    w_all, st_p, st_in, st_own, own_num, fac, ret, relay, ret_in, fin_out,
    loc_sem, meta_sem, ring_ss, ring_rs, a2a_ss, a2a_rs, x_ss, x_rs, m_ss, m_rs, st_ss, st_rs,
    ret_ss, ret_rs, fin_ss, fin_rs,
):
    r, k = lax.axis_index("req"), lax.axis_index("kv")
    x, z = r // nz, r % nz
    half = nz // 2
    rows2 = 2 * STEPS
    mid = nkv // 2
    sub = max(mid // 2, 1)
    parts = mid // sub

    def pair(i):
        return (k + 1 + i) % nkv

    def at_z(d):
        return (x * nz + (z + d + nz) % nz, k)

    def at_x(d):
        return (((x + d) % NX) * nz + z, k)

    def at_k(o):
        return (r, (k + o) % nkv)

    def remote(src, dst, ss, rs, dev):
        return pltpu.make_async_remote_copy(
            src_ref=src, dst_ref=dst, send_sem=ss, recv_sem=rs, device_id=dev, device_id_type=MESH
        )

    local = [
        pltpu.make_async_copy(pk_hbm, k_all.at[z, 0 : 2 * BLK], loc_sem.at[0]),
        pltpu.make_async_copy(pv_hbm, v_nat, loc_sem.at[1]),
        pltpu.make_async_copy(par_hbm, par_s, loc_sem.at[2]),
        pltpu.make_async_copy(owner_hbm, owner_s, loc_sem.at[3]),
        pltpu.make_async_copy(node_hbm, node_s, loc_sem.at[4]),
        pltpu.make_async_copy(len_hbm, len_s, loc_sem.at[5]),
        pltpu.make_async_copy(
            q_hbm.at[:, pl.ds(pl.multiple_of(k * (GROUP * HD), HD), GROUP * HD)], q_all.at[x, k], loc_sem.at[6]
        ),
        pltpu.make_async_copy(nk_hbm.at[:, pl.ds(pl.multiple_of(k * HD, HD), HD)], nk.at[k], loc_sem.at[7]),
        pltpu.make_async_copy(nv_hbm.at[:, pl.ds(pl.multiple_of(k * HD, HD), HD)], nv.at[k], loc_sem.at[8]),
        pltpu.make_async_copy(sk_hbm, sk, loc_sem.at[9]),
        pltpu.make_async_copy(sv_hbm, sv, loc_sem.at[10]),
    ]
    for c in local:
        c.start()

    barrier = pltpu.get_barrier_semaphore()
    trees = [block_tree(half, j) for j in JUMPS]
    jumps = sorted({abs(e - d) for tree, _ in trees for e, d in tree.items()})
    peers = [at_z(s * d) for d in jumps for s in (1, -1)] + [at_x(d) for d in range(1, NX)] + [at_k(o) for o in range(1, nkv)]
    for dev in peers:
        pl.semaphore_signal(barrier, inc=1, device_id=dev, device_id_type=MESH)
    local[2].wait()
    flag = jnp.where(par_s[1] == 0, 0.0, LOW).astype(F32)
    k_all[z, 2 * BLK : 2 * BLK + FLAG] = jnp.full((FLAG, HD), flag, F32).astype(BF16)
    local[0].wait()
    pl.semaphore_wait(barrier, len(peers))

    done = [lag + max(stage.values()) + 1 for lag, (_, stage) in zip(LAGS, trees)]
    def chunk(ref, lo, hi):
        return lambda b: ref.at[b, lo:hi]

    chunks = [
        (0, chunk(k_all, 0, BLK), 0),
        (1, chunk(k_all, BLK, 2 * BLK + FLAG), 0),
        (2, chunk(v_all, 0, HD // 2), 1),
        (3, chunk(v_all, HD // 2, HD), 1),
    ]

    def carried(c, dirn, d):
        return d < half or c % 2 == dirn

    def hand_on(c, at, tree, d, dirn):
        sign = 1 - 2 * dirn
        block = (z - sign * d + nz) % nz
        for e in sorted((e for e in tree if tree[e] == d), reverse=True):
            if carried(c, dirn, e):
                ref = at(block)
                remote(ref, ref, ring_ss.at[dirn, c, e], ring_rs.at[dirn, c, e], at_z(sign * (e - d))).start()

    def arrive(c, at, d, dirn):
        sign = 1 - 2 * dirn
        if carried(c, dirn, d):
            ref = at((z - sign * d + nz) % nz)
            remote(ref, ref, ring_ss.at[dirn, c, d], ring_rs.at[dirn, c, d], at_z(sign)).wait_recv()

    def slot(t, *kinds):
        for c, at, i in chunks:
            if kinds and i not in kinds:
                continue
            tree, stage = trees[i]
            for d in range(half + 1):
                if LAGS[i] + stage[d] != t:
                    continue
                for dirn in (0, 1):
                    if d > 0:
                        arrive(c, at, d, dirn)
                    hand_on(c, at, tree, d, dirn)

    def drain():
        for c, at, i in chunks:
            tree = trees[i][0]
            for d in range(1, half + 1):
                for dirn in (0, 1):
                    if carried(c, dirn, d):
                        ref = at((z - (1 - 2 * dirn) * tree[d] + nz) % nz)
                        remote(ref, ref, ring_ss.at[dirn, c, d], ring_rs.at[dirn, c, d], at_z(1)).wait_send()

    def a2a(i, o, got=False):
        to = (k + o) % nkv
        frm = (k + nkv - o) % nkv
        wide = pl.ds(pl.multiple_of(to * (GROUP * HD), HD), GROUP * HD)
        thin = pl.ds(pl.multiple_of(to * HD, HD), HD)
        src = (q_hbm.at[:, wide], nk_hbm.at[:, thin], nv_hbm.at[:, thin])[i]
        dst = (q_all.at[x], nk, nv)[i]
        if got:
            src, dst = dst.at[frm], dst.at[frm]
        else:
            dst = dst.at[k]
        return remote(src, dst, a2a_ss.at[i, o], a2a_rs.at[i, o], at_k(o))

    slot(0, 0)
    for i in range(3):
        for o in range(1, nkv):
            a2a(i, o).start()

    local[1].wait()
    v_all[z] = v_nat[...].astype(F32).T.astype(BF16)
    slot(0, 1)

    local[3].wait()
    local[4].wait()
    local[5].wait()
    lane = lax.broadcasted_iota(I32, (1, HD), 1)
    own_z = own_x = nodes = jnp.zeros((1, HD), I32)
    for i in range(2 * nkv):
        own_z = jnp.where(lane == i, owner_s[i] % nz, own_z)
        own_x = jnp.where(lane == i, owner_s[i] // nz, own_x)
        nodes = jnp.where(lane == i, node_s[i], nodes)
    pad = jnp.zeros((5, HD), I32)
    meta[x] = jnp.concatenate([own_z, own_x, nodes, pad], axis=0)
    for d in range(1, NX):
        remote(meta.at[x], meta.at[x], m_ss.at[d], m_rs.at[d], at_x(d)).start()

    first = (lane // STEPS) % 2 == 0

    def both(a, b):
        return jnp.where(first, a, b)

    def pair_queries(src, p):
        slab = q_all[src, p]
        return jnp.concatenate([slab[:, j * HD : (j + 1) * HD] for j in range(GROUP)], axis=0)

    def send_queries():
        for o in range(1, nkv):
            a2a(0, o, True).wait_recv()
        local[6].wait()
        for d in (1, 3, 2):
            remote(q_all.at[x], q_all.at[x], x_ss.at[d], x_rs.at[d], at_x(d)).start()

    def await_queries(d):
        src = (x + d) % NX
        remote(q_all.at[src], q_all.at[src], x_ss.at[NX - d], x_rs.at[NX - d], at_x(d)).wait_recv()

    def await_meta():
        for d in range(1, NX):
            src = (x + d) % NX
            remote(meta.at[src], meta.at[src], m_ss.at[NX - d], m_rs.at[NX - d], at_x(d)).wait_recv()
        c = pltpu.make_async_copy(meta, meta_s, meta_sem.at[0])
        c.start()
        c.wait()

    def await_own():
        for o in range(1, nkv):
            a2a(1, o, True).wait_recv()
            a2a(2, o, True).wait_recv()
        for i in (7, 8, 9, 10):
            local[i].wait()

    def own_pair(i):
        p = pair(i)
        queries = pair_queries(x, p)
        len_a, len_b = len_s[2 * p], len_s[2 * p + 1]
        s_suf = both(dot(sk[2 * p], queries, NT), dot(sk[2 * p + 1], queries, NT))
        s_new = dot(nk[p], queries, NT)
        pos = lax.broadcasted_iota(I32, (SUF, HD), 0)
        s_suf = jnp.where(pos < both(len_a, len_b), s_suf, LOW)
        row = lax.broadcasted_iota(I32, (rows2, HD), 0)
        col = lax.broadcasted_iota(I32, (rows2, HD), 1)
        seen = (row // STEPS == (col // STEPS) % 2) & (row % STEPS <= col % STEPS)
        s_new = jnp.where(seen, s_new, LOW)
        peak = jnp.maximum(jnp.max(s_suf, axis=0, keepdims=True), jnp.max(s_new, axis=0, keepdims=True))
        w_suf = jnp.exp2((s_suf - peak) * EXPO)
        w_new = jnp.exp2((s_new - peak) * EXPO)
        total = jnp.sum(w_suf, axis=0, keepdims=True) + jnp.sum(w_new, axis=0, keepdims=True)
        w_suf, w_new = w_suf.astype(BF16), w_new.astype(BF16)
        va = sv[2 * p].astype(F32).T.astype(BF16)
        vb = sv[2 * p + 1].astype(F32).T.astype(BF16)
        vn = nv[p].astype(F32).T.astype(BF16)
        own_num[i] = both(dot(va, w_suf), dot(vb, w_suf)) + dot(vn, w_new)
        st_own[0, i : i + 1] = peak
        st_own[1, i : i + 1] = total

    def prompt_weights(d, i):
        src, p = (x + d) % NX, pair(i)
        a, b = 2 * p, 2 * p + 1
        queries = pair_queries(src, p)
        ka, kb = meta_s[src, 0, a], meta_s[src, 0, b]
        node_a, node_b = meta_s[src, 2, a], meta_s[src, 2, b]
        s = both(dot(k_all[ka, 0 : 2 * BLK], queries, NT), dot(k_all[kb, 0 : 2 * BLK], queries, NT))
        flag_a = k_all[ka, 2 * BLK : 2 * BLK + FLAG].astype(F32)[0:1]
        flag_b = k_all[kb, 2 * BLK : 2 * BLK + FLAG].astype(F32)[0:1]
        nodes_ab = both(node_a, node_b)
        s0 = s[0:BLK] + jnp.where(nodes_ab == 1, both(flag_a, flag_b), 0.0)
        s1 = s[BLK:] + jnp.where(nodes_ab == 1, 0.0, LOW)
        peak = jnp.max(jnp.maximum(s0, s1), axis=0, keepdims=True)
        w0 = jnp.exp2((s0 - peak) * EXPO)
        w1 = jnp.exp2((s1 - peak) * EXPO)
        st_p[d, 0, i : i + 1] = peak
        st_p[d, 1, i : i + 1] = jnp.sum(w0 + w1, axis=0, keepdims=True)
        w_all[d, i, 0:BLK] = w0.astype(BF16)
        w_all[d, i, BLK:] = w1.astype(BF16)

    def send_stats(d):
        e = NX - d
        remote(st_p.at[d], st_in.at[e], st_ss.at[d], st_rs.at[e], at_x(d)).start()

    def prompt_values(d, i):
        src, p = (x + d) % NX, pair(i)
        w = w_all[d, i]
        num = both(dot(v_all[meta_s[src, 0, 2 * p]], w), dot(v_all[meta_s[src, 0, 2 * p + 1]], w))
        ret[d, i] = num.astype(BF16)

    def owner_side(src, i):
        p = pair(i)
        return both((meta_s[src, 1, 2 * p] - x + NX) % NX, (meta_s[src, 1, 2 * p + 1] - x + NX) % NX)

    def places(high, s):
        lo = high * mid + s * sub
        return slice(lo, lo + sub)

    routes = [
        (lambda s: ret.at[2, places(0, s)], lambda s: relay.at[0, s * sub : (s + 1) * sub], -1),
        (lambda s: ret.at[2, places(1, s)], lambda s: relay.at[1, s * sub : (s + 1) * sub], 1),
        (lambda s: ret.at[3, places(1, s)], lambda s: ret_in.at[0, places(1, s)], -1),
        (lambda s: ret.at[1, places(0, s)], lambda s: ret_in.at[1, places(0, s)], 1),
        (lambda s: ret.at[3, places(0, s)], lambda s: ret_in.at[0, places(0, s)], -1),
        (lambda s: ret.at[1, places(1, s)], lambda s: ret_in.at[1, places(1, s)], 1),
    ]

    def back(n, s):
        src, dst, step = routes[n]
        return remote(src(s), dst(s), ret_ss.at[n, s], ret_rs.at[n, s], at_x(step + NX))

    def arrived(n, s):
        dst = routes[n][1](s)
        remote(dst, dst, ret_ss.at[n, s], ret_rs.at[n, s], at_x(1)).wait_recv()

    def put_between(high, s):
        d, far = (1, 3) if high else (3, 1)
        for i in range(nkv)[places(high, s)]:
            there = owner_side((x + d) % NX, i) == far
            ret[d, i] = jnp.where(there, relay[high, i - high * mid].astype(F32), ret[d, i].astype(F32)).astype(BF16)

    def factors():
        for e in range(1, NX):
            remote(st_in.at[e], st_in.at[e], st_ss.at[e], st_rs.at[e], at_x(e)).wait_recv()
        for i in range(nkv):
            side = owner_side(x, i)
            row = slice(i, i + 1)
            peak, total = st_p[0, 0, row], st_p[0, 1, row]
            for e in range(1, NX):
                peak = jnp.where(side == e, st_in[e, 0, row], peak)
                total = jnp.where(side == e, st_in[e, 1, row], total)
            peak_own, total_own = st_own[0, row], st_own[1, row]
            top = jnp.maximum(peak, peak_own)
            f_p = jnp.exp2((peak - top) * EXPO)
            f_o = jnp.exp2((peak_own - top) * EXPO)
            inv = 1.0 / (f_p * total + f_o * total_own)
            fac[0, row] = f_p * inv
            fac[1, row] = f_o * inv

    def merge(i):
        side = owner_side(x, i)
        right = (side == 1) | (side == 2) if i < mid else side == 1
        num = jnp.where(right, ret_in[0, i].astype(F32), ret_in[1, i].astype(F32))
        num = jnp.where(side == 0, ret[0, i].astype(F32), num)
        out = num * fac[0, i : i + 1] + own_num[i] * fac[1, i : i + 1]
        fin_out[i] = out.astype(BF16)
        if i < nkv - 1:
            remote(fin_out.at[i], fin.at[k], fin_ss.at[i], fin_rs.at[i], (r, pair(i))).start()
        else:
            pltpu.make_async_copy(fin_out.at[i], fin.at[k], meta_sem.at[0]).start()

    def final(i):
        g = (k + 2 * nkv - 1 - i) % nkv
        remote(fin.at[g], fin.at[g], fin_ss.at[i], fin_rs.at[i], at_k(1)).wait_recv()

    last = max(done)
    before = {t: [] for t in range(1, last + 1)}

    def plan(t, f, *args):
        before[min(t, last)].append(functools.partial(f, *args))

    plan(2, send_queries)
    plan(3, await_own)
    for p in range(nkv):
        plan(3 + (p * 3) // nkv, own_pair, p)
    plan(min(6, done[0]), await_meta)

    def spread(work, start, end):
        for i, (d, p) in enumerate(work):
            t = start + (i * max(end - start, 1)) // len(work)
            yield t, d, p

    order = [(d, p) for d in (0, 1, 3, 2) for p in range(nkv)]
    for t, d, p in spread(order, done[0], done[1]):
        if p == 0 and d:
            plan(t, await_queries, d)
        plan(t, prompt_weights, d, p)
        if p == nkv - 1 and d:
            plan(t, send_stats, d)
    for t in range(1, last + 1):
        for f in before[t]:
            f()
        if t < last:
            slot(t)

    ways = [(high, s) for s in range(parts) for high in (0, 1)]
    for high, s in ways:
        for i in range(nkv)[places(high, s)]:
            prompt_values(2, i)
        back(high, s).start()
    for high, s in ways:
        d = 3 if high else 1
        for i in range(nkv)[places(high, s)]:
            prompt_values(d, i)
        back(2 if high else 3, s).start()
    for high, s in ways:
        d = 1 if high else 3
        for i in range(nkv)[places(high, s)]:
            prompt_values(d, i)
    for i in range(nkv):
        prompt_values(0, i)
    for high, s in ways:
        arrived(high, s)
        put_between(high, s)
        back(4 + high, s).start()
    factors()
    for high, s in ways:
        arrived(2 if high else 3, s)
    for high, s in ways:
        arrived(4 + high, s)
        for i in range(nkv)[places(high, s)]:
            merge(i)
    for high, s in ways:
        for i in range(nkv)[places(high, s)]:
            if i < nkv - 1:
                final(i)

    pltpu.make_async_copy(fin_out.at[nkv - 1], fin.at[k], meta_sem.at[0]).wait()

    drain()
    for o in range(1, nkv):
        for i in range(3):
            a2a(i, o).wait_send()
    for i in range(nkv - 1):
        remote(fin_out.at[i], fin.at[i], fin_ss.at[i], fin_rs.at[i], at_k(1)).wait_send()
    for d in range(1, NX):
        remote(q_all.at[x], q_all.at[x], x_ss.at[d], x_rs.at[d], at_x(d)).wait_send()
        remote(meta.at[x], meta.at[x], m_ss.at[d], m_rs.at[d], at_x(d)).wait_send()
        remote(st_p.at[d], st_in.at[d], st_ss.at[d], st_rs.at[d], at_x(d)).wait_send()
    for n in range(len(routes)):
        for s in range(parts):
            back(n, s).wait_send()


def finish(fin, out_ref):
    rows2 = 2 * STEPS
    for g in range(fin.shape[0]):
        rows = fin[g].astype(F32).T.astype(BF16)
        for j in range(GROUP):
            at = (g * GROUP + j) * HD
            out_ref[:, at : at + HD] = rows[j * rows2 : (j + 1) * rows2]


def solution(mesh):
    nz = mesh.shape["req"] // NX
    nkv = mesh.shape["kv"]
    half = nz // 2
    mid = nkv // 2
    parts = mid // max(mid // 2, 1)
    rows2 = 2 * STEPS

    def shards(q, nk, nv, sk, sv, length, pk, pv, parent, owner, node):
        q = q.reshape(rows2, -1)
        nk = nk.reshape(rows2, -1)
        nv = nv.reshape(rows2, -1)
        pk = pk.reshape(2 * BLK, HD)
        pv = pv.reshape(2 * BLK, HD)
        dma = pltpu.SemaphoreType.DMA
        vmem = pltpu.VMEM
        out = pl.pallas_call(
            functools.partial(kernel, nz, nkv),
            out_shape=jax.ShapeDtypeStruct((nkv, HD, HD), BF16),
            in_specs=[pl.BlockSpec(memory_space=pltpu.HBM)] * 11,
            out_specs=pl.BlockSpec(memory_space=pltpu.HBM),
            scratch_shapes=[
                vmem((nz, 2 * BLK + FLAG, HD), BF16),
                vmem((2 * BLK, HD), BF16),
                vmem((nz, HD, 2 * BLK), BF16),
                vmem((NX, nkv, rows2, GROUP * HD), BF16),
                vmem((nkv, rows2, HD), BF16),
                vmem((nkv, rows2, HD), BF16),
                vmem((2 * nkv, SUF, HD), BF16),
                vmem((2 * nkv, SUF, HD), BF16),
                vmem((NX, 8, HD), I32),
                pltpu.SMEM((NX, 8, HD), I32),
                pltpu.SMEM((2 * nkv,), I32),
                pltpu.SMEM((2,), I32),
                pltpu.SMEM((2 * nkv,), I32),
                pltpu.SMEM((2 * nkv,), I32),
                vmem((NX, nkv, 2 * BLK, HD), BF16),
                vmem((NX, 2, nkv, HD), F32),
                vmem((NX, 2, nkv, HD), F32),
                vmem((2, nkv, HD), F32),
                vmem((nkv, HD, HD), F32),
                vmem((2, nkv, HD), F32),
                vmem((NX, nkv, HD, HD), BF16),
                vmem((2, mid, HD, HD), BF16),
                vmem((2, nkv, HD, HD), BF16),
                vmem((nkv, HD, HD), BF16),
                dma((11,)),
                dma((1,)),
                dma((2, 4, half + 1)),
                dma((2, 4, half + 1)),
                dma((3, nkv)),
                dma((3, nkv)),
                dma((NX,)),
                dma((NX,)),
                dma((NX,)),
                dma((NX,)),
                dma((NX,)),
                dma((NX,)),
                dma((6, parts)),
                dma((6, parts)),
                dma((nkv,)),
                dma((nkv,)),
            ],
            compiler_params=pltpu.CompilerParams(
                collective_id=0, has_side_effects=True, vmem_limit_bytes=60 * 2**20
            ),
        )(q, nk, nv, sk, sv, pk, pv, length, parent, owner, node)
        out = pl.pallas_call(
            finish,
            grid=(2,),
            in_specs=[pl.BlockSpec((nkv // 2, HD, HD), lambda i: (i, 0, 0))],
            out_specs=pl.BlockSpec((rows2, nkv // 2 * GROUP * HD), lambda i: (0, i)),
            out_shape=jax.ShapeDtypeStruct((rows2, nkv * GROUP * HD), BF16),
        )(out)
        return out.reshape(2, STEPS, -1)

    in_specs = (
        P(("req", "kv"), None, None),
        P(("req", "kv"), None, None),
        P(("req", "kv"), None, None),
        P("req", None, "kv"),
        P("req", None, "kv"),
        P("req"),
        P("req", None, "kv"),
        P("req", None, "kv"),
        P("req"),
        P("req"),
        P("req"),
    )
    return jax.shard_map(
        shards, mesh=mesh, in_specs=in_specs, out_specs=P(("req", "kv"), None, None), check_vma=False
    )
```

time: 76.4 us -> 60.5 us (0.79)
  Pallas kernels: 68.5 us -> 60.3 us
  local copies, waits for them, and re-layouts: 7.44 us -> 0 us
    pallas_call x1, Pallas kernels: 68.5 us -> 58.5 us  [shards(): pl.pallas_call(functools.partial(kernel, nz, nkv), out_shape=jax.ShapeDty...]
    unnamed x23 -> x0, local copies, waits for them, and re-layouts: 7.44 us -> none
    pallas_call x0 -> x1, Pallas kernels: none -> 1.8 us  [shards(): pl.pallas_call(finish, grid=(2,), in_specs=[pl.BlockSpec((nkv // 2, HD, H...]
where the time goes in v2:
time: 60.5 us; the launch traced here: 60.3 us
  Pallas kernels  60.3 us (100%)
    pallas_call x1, Pallas kernels, shards(): pl.pallas_call(functools.partial(kernel, nz, nkv), out_shape=jax.ShapeDty...  58.5 us
    pallas_call x1, Pallas kernels, shards(): pl.pallas_call(finish, grid=(2,), in_specs=[pl.BlockSpec((nkv // 2, HD, H...  1.8 us

profile of v2, /device:TPU:1, one launch (start us, length us, event | category | flops | bytes accessed | tf_op | source)
XLA Modules:
  0.0 60.3 jit_solution(17801160300304656113)
XLA Ops:
  0.0 58.5 %shard_map.109.fin = bf16[8,128,128]{2,1,0:T(8,128)(2,1)} custom-call(bf16[16,8192]{1,0:T(8,128)(2,1)} %bitcast.6, bf16[16,1024]{1,0:T(8,128)(2,1)} %bitcast.9, bf16[16,1024]{1,0:T(8,128)(2,1)} %bitcast.10, bf16[16,64,128]{2,1,0:T(8,128)(2,1)} %sk_hbm.1, bf16[16,64,128]{2,1,0:T(8,128)(2,1)} %sv_hbm.1, bf16[256,128]{1,0:T(8,128)(2,1)} %bitcast.7, ...), custom_call_target="tpu_custom_call" | custom-call | tf_op jit(solution)/shard_map/pallas_call | solution.py:454
  58.5 1.8 %shard_map.110 = bf16[16,8192]{1,0:T(8,128)(2,1)} custom-call(bf16[8,128,128]{2,1,0:T(8,128)(2,1)} %shard_map.109.fin), custom_call_target="tpu_custom_call" | custom-call | tf_op jit(solution)/shard_map/pallas_call | solution.py:505

commit v3 on v2

--- a/solution.py
+++ b/solution.py
@@ -45,10 +45,10 @@
 def kernel(
     nz, nkv,
     q_hbm, nk_hbm, nv_hbm, sk_hbm, sv_hbm, pk_hbm, pv_hbm, len_hbm, par_hbm, owner_hbm, node_hbm,
-    fin,
+    out_ref,
     k_all, v_nat, v_all, q_all, nk, nv, sk, sv,
     meta, meta_s, len_s, par_s, owner_s, node_s,
-    w_all, st_p, st_in, st_own, own_num, fac, ret, relay, ret_in, fin_out,
+    w_all, st_p, st_in, st_own, own_num, fac, ret, relay, ret_in, fin_out, fin,
     loc_sem, meta_sem, ring_ss, ring_rs, a2a_ss, a2a_rs, x_ss, x_rs, m_ss, m_rs, st_ss, st_rs,
     ret_ss, ret_rs, fin_ss, fin_rs,
 ):
@@ -57,7 +57,7 @@
     half = nz // 2
     rows2 = 2 * STEPS
     mid = nkv // 2
-    sub = max(mid // 2, 1)
+    sub = max(mid // 4, 1)
     parts = mid // sub
 
     def pair(i):
@@ -105,6 +105,8 @@
     flag = jnp.where(par_s[1] == 0, 0.0, LOW).astype(F32)
     k_all[z, 2 * BLK : 2 * BLK + FLAG] = jnp.full((FLAG, HD), flag, F32).astype(BF16)
     local[0].wait()
+    local[1].wait()
+    v_all[z] = v_nat[...].astype(F32).T.astype(BF16)
     pl.semaphore_wait(barrier, len(peers))
 
     done = [lag + max(stage.values()) + 1 for lag, (_, stage) in zip(LAGS, trees)]
@@ -135,10 +137,8 @@
             ref = at((z - sign * d + nz) % nz)
             remote(ref, ref, ring_ss.at[dirn, c, d], ring_rs.at[dirn, c, d], at_z(sign)).wait_recv()
 
-    def slot(t, *kinds):
+    def slot(t):
         for c, at, i in chunks:
-            if kinds and i not in kinds:
-                continue
             tree, stage = trees[i]
             for d in range(half + 1):
                 if LAGS[i] + stage[d] != t:
@@ -170,14 +170,10 @@
             dst = dst.at[k]
         return remote(src, dst, a2a_ss.at[i, o], a2a_rs.at[i, o], at_k(o))
 
-    slot(0, 0)
+    slot(0)
     for i in range(3):
         for o in range(1, nkv):
             a2a(i, o).start()
-
-    local[1].wait()
-    v_all[z] = v_nat[...].astype(F32).T.astype(BF16)
-    slot(0, 1)
 
     local[3].wait()
     local[4].wait()
@@ -339,13 +335,19 @@
         out = num * fac[0, i : i + 1] + own_num[i] * fac[1, i : i + 1]
         fin_out[i] = out.astype(BF16)
         if i < nkv - 1:
-            remote(fin_out.at[i], fin.at[k], fin_ss.at[i], fin_rs.at[i], (r, pair(i))).start()
+            remote(fin_out.at[i], fin.at[i], fin_ss.at[i], fin_rs.at[i], (r, pair(i))).start()
+
+    def final(i):
+        if i < nkv - 1:
+            remote(fin.at[i], fin.at[i], fin_ss.at[i], fin_rs.at[i], at_k(1)).wait_recv()
+            rows = fin[i]
         else:
-            pltpu.make_async_copy(fin_out.at[i], fin.at[k], meta_sem.at[0]).start()
-
-    def final(i):
+            rows = fin_out[i]
+        rows = rows.astype(F32).T.astype(BF16)
         g = (k + 2 * nkv - 1 - i) % nkv
-        remote(fin.at[g], fin.at[g], fin_ss.at[i], fin_rs.at[i], at_k(1)).wait_recv()
+        for j in range(GROUP):
+            at = pl.ds(pl.multiple_of((g * GROUP + j) * HD, HD), HD)
+            out_ref[:, at] = rows[j * rows2 : (j + 1) * rows2]
 
     last = max(done)
     before = {t: [] for t in range(1, last + 1)}
@@ -404,12 +406,11 @@
         arrived(4 + high, s)
         for i in range(nkv)[places(high, s)]:
             merge(i)
+    final(nkv - 1)
     for high, s in ways:
         for i in range(nkv)[places(high, s)]:
             if i < nkv - 1:
                 final(i)
-
-    pltpu.make_async_copy(fin_out.at[nkv - 1], fin.at[k], meta_sem.at[0]).wait()
 
     drain()
     for o in range(1, nkv):
@@ -426,21 +427,12 @@
             back(n, s).wait_send()
 
 
-def finish(fin, out_ref):
-    rows2 = 2 * STEPS
-    for g in range(fin.shape[0]):
-        rows = fin[g].astype(F32).T.astype(BF16)
-        for j in range(GROUP):
-            at = (g * GROUP + j) * HD
-            out_ref[:, at : at + HD] = rows[j * rows2 : (j + 1) * rows2]
-
-
 def solution(mesh):
     nz = mesh.shape["req"] // NX
     nkv = mesh.shape["kv"]
     half = nz // 2
     mid = nkv // 2
-    parts = mid // max(mid // 2, 1)
+    parts = mid // max(mid // 4, 1)
     rows2 = 2 * STEPS
 
     def shards(q, nk, nv, sk, sv, length, pk, pv, parent, owner, node):
@@ -450,12 +442,16 @@
         pk = pk.reshape(2 * BLK, HD)
         pv = pv.reshape(2 * BLK, HD)
         dma = pltpu.SemaphoreType.DMA
+        q, nk, nv, sk, sv, pk, pv, length, parent, owner, node = (
+            pltpu.with_memory_space_constraint(a, pltpu.HBM)
+            for a in (q, nk, nv, sk, sv, pk, pv, length, parent, owner, node)
+        )
         vmem = pltpu.VMEM
         out = pl.pallas_call(
             functools.partial(kernel, nz, nkv),
-            out_shape=jax.ShapeDtypeStruct((nkv, HD, HD), BF16),
+            out_shape=jax.ShapeDtypeStruct((rows2, nkv * GROUP * HD), BF16),
             in_specs=[pl.BlockSpec(memory_space=pltpu.HBM)] * 11,
-            out_specs=pl.BlockSpec(memory_space=pltpu.HBM),
+            out_specs=pl.BlockSpec(memory_space=pltpu.VMEM),
             scratch_shapes=[
                 vmem((nz, 2 * BLK + FLAG, HD), BF16),
                 vmem((2 * BLK, HD), BF16),
@@ -481,6 +477,7 @@
                 vmem((2, mid, HD, HD), BF16),
                 vmem((2, nkv, HD, HD), BF16),
                 vmem((nkv, HD, HD), BF16),
+                vmem((nkv, HD, HD), BF16),
                 dma((11,)),
                 dma((1,)),
                 dma((2, 4, half + 1)),
@@ -499,16 +496,9 @@
                 dma((nkv,)),
             ],
             compiler_params=pltpu.CompilerParams(
-                collective_id=0, has_side_effects=True, vmem_limit_bytes=60 * 2**20
+                collective_id=0, has_side_effects=True, vmem_limit_bytes=32 * 2**20
             ),
         )(q, nk, nv, sk, sv, pk, pv, length, parent, owner, node)
-        out = pl.pallas_call(
-            finish,
-            grid=(2,),
-            in_specs=[pl.BlockSpec((nkv // 2, HD, HD), lambda i: (i, 0, 0))],
-            out_specs=pl.BlockSpec((rows2, nkv // 2 * GROUP * HD), lambda i: (0, i)),
-            out_shape=jax.ShapeDtypeStruct((rows2, nkv * GROUP * HD), BF16),
-        )(out)
         return out.reshape(2, STEPS, -1)
 
     in_specs = (

time: 60.5 us -> 59.4 us (0.982)
  Pallas kernels: 60.3 us -> 58.6 us
  local copies, waits for them, and re-layouts: 0 us -> 0.71 us
    pallas_call x1 -> x0, Pallas kernels: 1.8 us -> none  [shards(): pl.pallas_call(finish, grid=(2,), in_specs=[pl.BlockSpec((nkv // 2, HD, H...]
    unnamed x0 -> x1, local copies, waits for them, and re-layouts: none -> 0.71 us
where the time goes in v3:
time: 59.4 us; the launch traced here: 59.3 us
  Pallas kernels  58.6 us (99%)
  local copies, waits for them, and re-layouts  0.71 us (1%)
    pallas_call x1, Pallas kernels, shards(): pl.pallas_call(functools.partial(kernel, nz, nkv), out_shape=jax.ShapeDty...  58.6 us

profile of v3, /device:TPU:1, one launch (start us, length us, event | category | flops | bytes accessed | tf_op | source)
XLA Modules:
  0.0 59.3 jit_solution(7596430656206145198)
XLA Ops:
  0.0 58.6 %shard_map.109 = bf16[16,8192]{1,0:T(8,128)(2,1)S(1)} custom-call(bf16[16,8192]{1,0:T(8,128)(2,1)} %bitcast.7, bf16[16,1024]{1,0:T(8,128)(2,1)} %bitcast.10, bf16[16,1024]{1,0:T(8,128)(2,1)} %bitcast.11, bf16[16,64,128]{2,1,0:T(8,128)(2,1)} %sk_hbm.1, bf16[16,64,128]{2,1,0:T(8,128)(2,1)} %sv_hbm.1, bf16[256,128]{1,0:T(8,128)(2,1)} %bitcast.8, ...), custom_call_target="tpu_custom_call" | custom-call | tf_op jit(solution)/shard_map/pallas_call | solution.py:450
  58.6 0.7 %copy.13 = bf16[2,8,8192]{2,1,0:T(8,128)(2,1)} copy(bf16[2,8,8192]{2,1,0:T(8,128)(2,1)S(1)} %bitcast.6) | data formatting | bytes 524288
